TPU v7x, 512 devices: a whole 4x4x16 slice. The times are simulated.
512 devices in a mesh: dp: 8 (over z_lo), group: 4 (over x), head: 16 (over y, z_hi, core).
Axes of the slice: x: 4, y: 4, z: 16 (z_hi: 2, z_lo: 8; z = z_hi * 8 + z_lo), core: 2. Of those that a mesh axis runs over, the one named last changes fastest.
Arguments:
- query: bfloat16 [16384, 8192], P('dp', ('group', 'head')), parts along dimension 0, may hold values from -200 to 200
- query_exp: int32 [256, 16384], P(('group', 'head'), 'dp'), parts along dimension 1, may hold values from -1 to 0
- kv: bfloat16 [16384, 1024], P('dp', 'group'), parts along dimension 0, may hold values from -10 to 10
- kv_exp: int32 [32, 16384], P('group', 'dp'), parts along dimension 1, may hold values from -2 to 2, as said below
- out_grad: bfloat16 [16384, 8192], P('dp', ('group', 'head')), parts along dimension 0, may hold values from -6 to 6
- out_grad_exp: int32 [256, 16384], P(('group', 'head'), 'dp'), parts along dimension 1, may hold values from -2 to 2
- q_weight: bfloat16 [16384, 8192], P('dp', ('group', 'head')), parts along dimension 0, may hold values from -0.1875 to 0.1875
- q_weight_exp: int32 [512, 8192], P('dp', ('group', 'head')), parts along dimension 0, may hold values from -1 to 1
- keyvalue_weight_mantissa: bfloat16 [16384, 1024], P(('dp', 'head'), 'group'), parts along dimension 0, may hold values from -0.375 to 0.375
- keyvalue_weight_exponent: int32 [512, 1024], P(('dp', 'head'), 'group'), parts along dimension 0, may hold values from -1 to 1
Outputs:
- input_grad: bfloat16 [16384, 2048], P(('dp', 'head'), 'group'), parts along dimension 0
- keyvalue_gradient: bfloat16 [16384, 1024], P(('dp', 'head'), 'group'), parts along dimension 0
There are 8 independent parts, one for each index of `dp`. A program takes and returns all parts, laid end to end along the dimension named above; each array names one. Nothing has to cross between parts.
Inputs may be any that keep to these rules, and one draw needn't show every extreme that they name: `kv_exp`: exponents of the key blocks lie in -1 to 0, those of the value blocks in -2 to 2.
All inputs are finite; a program needn't handle non-finite values.
Results may differ from a plain program's by a relative error of at most 0.022.
Values may be sent and summed in bfloat16 or wider, within the bound.
No kernel may reach another device: no remote copies, remote signals or barrier semaphores. Data moves between devices by JAX's collectives and lax.ppermute only.
A program may use at most 64 MiB of HBM per device.

v0:
```python
import jax
import jax.numpy as jnp
from jax import lax
from jax.sharding import PartitionSpec as P


def power_of_two(block_exponent):
    scale_lookup = jnp.zeros(block_exponent.shape, jnp.float32)
    for level in range(-4, 5):
        scale_lookup = scale_lookup + jnp.where(block_exponent == level, 2.0**level, 0.0).astype(
            jnp.float32
        )
    return scale_lookup


def dequant_rows(mantissa, block_exponent):
    scaling = jnp.repeat(power_of_two(block_exponent).T, 32, axis=1)
    return (mantissa.astype(jnp.float32) * scaling).astype(jnp.bfloat16)


def dequant_cols(mantissa, block_exponent):
    scaling = jnp.repeat(power_of_two(block_exponent), 32, axis=0)
    return (mantissa.astype(jnp.float32) * scaling).astype(jnp.bfloat16)


def shards(
    query,
    query_exp,
    kv,
    kv_exp,
    out_grad,
    out_grad_exp,
    q_weight,
    q_weight_exp,
    keyvalue_weight_mantissa,
    keyvalue_weight_exponent,
):
    seq_len = query.shape[0]
    head_dim = query.shape[1]
    scale = 1.0 / head_dim**0.5
    q_local = dequant_rows(query, query_exp)
    kv_local = dequant_rows(kv, kv_exp)
    do_local = dequant_rows(out_grad, out_grad_exp)
    keys = kv_local[:, :head_dim]
    value_matrix = kv_local[:, head_dim:]
    block = min(512, seq_len)
    blocks = seq_len // block
    dq_parts = []
    dk_accum = jnp.zeros((seq_len, head_dim), jnp.float32)
    dv_accum = jnp.zeros((seq_len, head_dim), jnp.float32)
    for index in range(blocks):
        first = index * block
        upper = first + block
        q_block = q_local[first:upper]
        do_block = do_local[first:upper]
        key_rows = keys[:upper]
        value_rows = value_matrix[:upper]
        scores = (
            lax.dot_general(
                q_block, key_rows, (((1,), (1,)), ((), ())), preferred_element_type=jnp.float32
            )
            * scale
        )
        row_pos = first + jnp.arange(block, dtype=jnp.int32)[:, None]
        col_pos = jnp.arange(upper, dtype=jnp.int32)[None, :]
        scores = jnp.where(col_pos <= row_pos, scores, -jnp.inf)
        peak = jnp.max(scores, axis=1, keepdims=True)
        expd = jnp.exp(scores - peak)
        probs = expd / jnp.sum(expd, axis=1, keepdims=True)
        probs_b = probs.astype(jnp.bfloat16)
        output = jnp.dot(probs_b, value_rows, preferred_element_type=jnp.float32)
        delta = jnp.sum(do_block.astype(jnp.float32) * output, axis=1, keepdims=True)
        dprob = lax.dot_general(
            do_block, value_rows, (((1,), (1,)), ((), ())), preferred_element_type=jnp.float32
        )
        dscore = (probs * (dprob - delta) * scale).astype(jnp.bfloat16)
        dq_parts.append(
            jnp.dot(dscore, key_rows, preferred_element_type=jnp.float32).astype(jnp.bfloat16)
        )
        dk_accum = dk_accum.at[:upper].add(
            lax.dot_general(
                dscore, q_block, (((0,), (0,)), ((), ())), preferred_element_type=jnp.float32
            )
        )
        dv_accum = dv_accum.at[:upper].add(
            lax.dot_general(
                probs_b, do_block, (((0,), (0,)), ((), ())), preferred_element_type=jnp.float32
            )
        )
    dq_local = jnp.concatenate(dq_parts, axis=0)
    dkv_local = jnp.concatenate(
        [dk_accum.astype(jnp.bfloat16), dv_accum.astype(jnp.bfloat16)], axis=1
    )
    packed = jnp.concatenate([dq_local, dkv_local], axis=1)[:, None, :]
    moved = lax.all_to_all(packed, "head", split_axis=0, concat_axis=1, tiled=True)
    tok_rows = moved.shape[0]
    sources = moved.shape[1]
    dq_tokens = moved[:, :, :head_dim].reshape(tok_rows, sources * head_dim)
    kv_sum = jnp.sum(moved[:, :, head_dim:].astype(jnp.float32), axis=1)
    keyvalue_gradient = kv_sum.astype(jnp.bfloat16)
    w_query = dequant_cols(q_weight, q_weight_exp)
    total = lax.dot_general(
        dq_tokens,
        lax.all_gather(w_query, "head", axis=1, tiled=True),
        (((1,), (1,)), ((), ())),
        preferred_element_type=jnp.float32,
    )
    w_keyval = dequant_cols(keyvalue_weight_mantissa, keyvalue_weight_exponent)
    whole_keyval = lax.all_gather(w_keyval, "head", axis=0, tiled=True)
    total = total + lax.dot_general(
        keyvalue_gradient,
        whole_keyval,
        (((1,), (1,)), ((), ())),
        preferred_element_type=jnp.float32,
    )
    input_grad = lax.psum_scatter(
        total.astype(jnp.bfloat16), "group", scatter_dimension=1, tiled=True
    )
    return (input_grad, keyvalue_gradient)


def solution(mesh):
    return jax.shard_map(
        shards,
        mesh=mesh,
        in_specs=(
            P("dp", ("group", "head")),
            P(("group", "head"), "dp"),
            P("dp", "group"),
            P("group", "dp"),
            P("dp", ("group", "head")),
            P(("group", "head"), "dp"),
            P("dp", ("group", "head")),
            P("dp", ("group", "head")),
            P(("dp", "head"), "group"),
            P(("dp", "head"), "group"),
        ),
        out_specs=(P(("dp", "head"), "group"), P(("dp", "head"), "group")),
        check_vma=False,
    )
```

profile of v0, /device:TPU:8, one launch (start us, length us, event | category | flops | bytes accessed | tf_op | source)
XLA Modules:
  0.0 347.8 jit_solution(5404532560572737366)
XLA Ops:
  7.2 0.9 select_add_fusion
  8.1 2.0 fusion.26
  10.1 1.0 add_bitcast_fusion
  11.1 0.8 add_bitcast_fusion.2
  11.9 0.6 copy.52
  12.6 0.2 copy.51
  12.8 0.2 copy.53
  13.0 0.2 fusion.13
  13.3 0.1 fusion.28
  13.4 0.2 copy-done.6
  13.6 0.1 add_bitcast_fusion.1
  13.6 0.1 fusion.27
  13.7 0.4 fusion.75
  14.1 0.2 fusion.32
  14.3 0.2 fusion.45
  14.5 0.3 fusion.70
  14.8 0.1 scatter-add.25
  14.9 0.2 fusion.25
  15.1 0.4 fusion.19
  15.5 0.3 fusion.61
  15.8 0.1 scatter-add.20
  15.9 0.6 fusion.76
  16.5 0.5 fusion.15
  17.0 0.4 convolution_convert_fusion.1
  17.4 0.8 fusion.77
  18.2 0.6 fusion.7
  18.8 0.7 fusion.6
  19.4 0.7 fusion.22
  20.1 0.6 fusion.23
  20.8 0.7 multiply_convert_fusion.1
  21.5 0.4 convolution_convert_fusion.2
  21.9 0.6 fusion.5
  22.5 0.6 convolution_convert_fusion.3
  23.1 0.5 fusion.21
  23.6 1.0 fusion.78
  24.7 0.7 fusion.1
  25.4 0.8 fusion
  26.2 0.9 fusion.24
  27.1 1.0 multiply_convert_fusion
  28.0 0.7 convolution_convert_fusion
  28.7 0.7 fusion.9
  29.5 0.8 fusion.11
  30.3 0.8 fusion.20
  31.0 0.7 fusion.8
  31.7 0.8 fusion.12
  32.5 0.2 maximum_bitcast_fusion
  32.7 0.5 broadcast.219
  33.2 1.9 reduce.19
  35.1 1.4 reshape.246
  36.5 18.3 %all-to-all-start = ((bf16[16,2,24576]{2,1,0:T(2,128)(2,1)}), bf16[16,2,24576]{2,1,0:T(2,128)(2,1)}, u32[]{:S(2)}, u32[]{:S(2)}) async-start(bf16[16,2,24576]{2,1,0:T(2,128)(2,1)} %reshape.246), calls=%async_computation | async-start | bytes 3145728 | tf_op jit(solution)/shard_map/all_to_all | solution.py:95
  54.9 0.6 fusion.50
  55.6 0.0 reduce-scatter.2.cloned.1.call-start
  55.6 139.3 %all-to-all-done = bf16[16,2,24576]{2,1,0:T(2,128)(2,1)} async-done(((bf16[16,2,24576]{2,1,0:T(2,128)(2,1)}), bf16[16,2,24576]{2,1,0:T(2,128)(2,1)}, u32[]{:S(2)}, u32[]{:S(2)}) %all-to-all-start) | async-done | bytes 1572896 | tf_op jit(solution)/shard_map/all_to_all | solution.py:95
  195.0 8.1 %reshape.247 = bf16[2048,1,384]{2,1,0:T(2,128)(2,1)S(1)} reshape(bf16[16,2,24576]{2,1,0:T(2,128)(2,1)} %all-to-all-done) | data formatting | bytes 3145728
  203.1 0.3 copy.76
  203.3 1.2 copy-done
  204.6 0.1 slice.236
  204.7 0.3 copy.64
  204.9 1.4 slice_reduce_fusion
  206.3 37.9 %all-gather.3.cloned.1.call-done = bf16[2048,2048]{1,0:T(8,128)(2,1)} async-done(((bf16[2048,128]{1,0:T(8,128)(2,1)}), bf16[2048,2048]{1,0:T(8,128)(2,1)}) %all-gather.3.cloned.1.call-update) | async-done | bytes 8388624 | tf_op jit(solution)/shard_map/all_gather | solution.py:104
  244.2 6.3 %fusion.79 = f32[128,2048]{1,0:T(8,128)S(1)} fusion(bf16[128,2048]{0,1:T(8,128)(2,1)S(1)} %bitcast.50, bf16[2048,2048]{1,0:T(8,128)(2,1)} %all-gather.3.cloned.1.call-done), kind=kOutput, calls=%fused_computation.123 | convolution fusion | flops 1073741824 | bytes 9961472 | tf_op jit(solution)/shard_map/dot_general | solution.py:102
  250.6 67.1 %all-gather.5.cloned.1.call-done = bf16[2048,256]{1,0:T(8,128)(2,1)} async-done(((bf16[128,256]{1,0:T(8,128)(2,1)}), bf16[2048,256]{1,0:T(8,128)(2,1)}) %all-gather.5.cloned.1.call-update) | async-done | bytes 1048592 | tf_op jit(solution)/shard_map/all_gather | solution.py:109
  317.7 2.5 fusion.10
  320.2 21.1 %reduce-scatter.2.cloned.1.call-done = bf16[128,512]{1,0:T(8,128)(2,1)} async-done(((bf16[128,2048]{1,0:T(8,128)(2,1)}), bf16[128,512]{1,0:T(8,128)(2,1)}) %reduce-scatter.2.cloned.1.call-update) | async-done | bytes 131088 | tf_op jit(solution)/shard_map/reduce_scatter | solution.py:116
  (23 shorter events, 0.2 us)
Async XLA Ops:
  7.2 4.7 %copy-start.1 = (bf16[2048,256]{1,0:T(8,128)(2,1)S(1)}, bf16[2048,256]{1,0:T(8,128)(2,1)}, u32[]{:S(2)}) copy-start(bf16[2048,256]{1,0:T(8,128)(2,1)} %param.32) | copy-start | bytes 3145732
  7.2 5.4 %copy-start.2 = (bf16[2048,128]{1,0:T(8,128)(2,1)S(1)}, bf16[2048,128]{1,0:T(8,128)(2,1)}, u32[]{:S(2)}) copy-start(bf16[2048,128]{1,0:T(8,128)(2,1)} %param.30) | copy-start | bytes 1572868
  7.2 237.1 %all-gather.3.cloned.1.call-start = ((), (), s32[]{:S(2)}) async-start(), calls=%async_computation.2 | async-start | bytes 8912896 | tf_op jit(solution)/shard_map/all_gather | solution.py:104
  10.1 2.7 copy-start.3
  12.8 0.8 copy-start.6
  36.5 18.4 %copy-start.7 = (s32[4,256]{1,0:T(4,128)S(1)}, s32[4,256]{1,0:T(4,128)}, u32[]{:S(2)}) copy-start(s32[4,256]{1,0:T(4,128)} %param.39) | copy-start | bytes 12292
  36.5 18.4 %copy-start.5 = (bf16[128,256]{1,0:T(8,128)(2,1)S(1)}, bf16[128,256]{1,0:T(8,128)(2,1)}, u32[]{:S(2)}) copy-start(bf16[128,256]{1,0:T(8,128)(2,1)} %param.38) | copy-start | bytes 196612
  36.5 158.5 %all-to-all-start = ((bf16[16,2,24576]{2,1,0:T(2,128)(2,1)}), bf16[16,2,24576]{2,1,0:T(2,128)(2,1)}, u32[]{:S(2)}, u32[]{:S(2)}) async-start(bf16[16,2,24576]{2,1,0:T(2,128)(2,1)} %reshape.246), calls=%async_computation | async-start | bytes 3145728 | tf_op jit(solution)/shard_map/all_to_all | solution.py:95
  54.8 262.9 %all-gather.5.cloned.1.call-start = ((), (), s32[]{:S(2)}) async-start(), calls=%async_computation.3 | async-start | bytes 1114112 | tf_op jit(solution)/shard_map/all_gather | solution.py:109
  55.6 285.7 %reduce-scatter.2.cloned.1.call-start = ((), (), s32[]{:S(2)}) async-start(), calls=%async_computation.4 | async-start | bytes 655360 | tf_op jit(solution)/shard_map/reduce_scatter | solution.py:116
  203.3 1.2 copy-start
  206.3 111.4 %copy-start.4 = (bf16[128,256]{1,0:T(8,128)(2,1)}, bf16[128,256]{1,0:T(8,128)(2,1)S(1)}, u32[]{:S(2)}) copy-start(bf16[128,256]{1,0:T(8,128)(2,1)S(1)} %slice_reduce_fusion) | copy-start | bytes 196612
Sparse Core Ops, SparseCore 0:
  11.1 233.0 all-gather.2
  248.1 69.5 all-gather.4
  321.1 20.1 reduce-scatter.1
where the time goes:
time: 349 us; the launch traced here: 348 us
  waiting for transfers between devices  266 us (76%)
  matrix products  23.6 us (7%)
  starting transfers between devices  18.4 us (5%)
  between operations  14.1 us (4%)
  local copies, waits for them, and re-layouts  13.2 us (4%)
  other arithmetic  13 us (4%)
    all_to_all x1, waiting for transfers between devices, shards(): lax.all_to_all(packed, 'head', split_axis=0, concat_axis=1, tiled=True)  139 us
    all_gather x1, waiting for transfers between devices, shards(): whole_keyval = lax.all_gather(w_keyval, 'head', axis=0, tiled=True)  67.1 us
    all_gather x1, waiting for transfers between devices, shards(): lax.all_gather(w_query, 'head', axis=1, tiled=True)  37.9 us
    reduce_scatter x1, waiting for transfers between devices, shards(): lax.psum_scatter(total.astype(jnp.bfloat16), 'group', scatter_dimension=1...  21.1 us
    all_to_all x1, starting transfers between devices, shards(): lax.all_to_all(packed, 'head', split_axis=0, concat_axis=1, tiled=True)  18.3 us
    unnamed x22, local copies, waits for them, and re-layouts  12.2 us
  transfers between devices with their start and end apart: 4, of which 4 were waited for; matrix products, arithmetic and copies ran while one was open for 12% of the time, Pallas kernels for 0%

commit v1 on v0

--- a/solution.py
+++ b/solution.py
@@ -101,7 +101,9 @@
     w_query = dequant_cols(q_weight, q_weight_exp)
     total = lax.dot_general(
         dq_tokens,
-        lax.all_gather(w_query, "head", axis=1, tiled=True),
+        jnp.concatenate(
+            lax.all_to_all(jnp.stack([w_query] * lax.axis_size("head")), "head", 0, 0), axis=1
+        ),
         (((1,), (1,)), ((), ())),
         preferred_element_type=jnp.float32,
     )

time: 349 us -> 560 us (1.60)
  waiting for transfers between devices: 266 us -> 466 us
  starting transfers between devices: 18.4 us -> 26.2 us
  local copies, waits for them, and re-layouts: 13.2 us -> 19.5 us
    all_gather x1, waiting for transfers between devices: 67.1 us -> 288 us  [shards(): whole_keyval = lax.all_gather(w_keyval, 'head', axis=0, tiled=True)]
    all_to_all x0 -> x1, waiting for transfers between devices: none -> 107 us  [shards(): lax.all_to_all(jnp.stack([w_query] * lax.axis_size('head')), 'head', 0, 0)]
    all_to_all x1, waiting for transfers between devices: 139 us -> 37.6 us  [shards(): lax.all_to_all(packed, 'head', split_axis=0, concat_axis=1, tiled=True)]
    all_gather x1 -> x0, waiting for transfers between devices: 37.9 us -> none  [shards(): lax.all_gather(w_query, 'head', axis=1, tiled=True)]
    reduce_scatter x1, waiting for transfers between devices: 21.1 us -> 33.2 us  [shards(): lax.psum_scatter(total.astype(jnp.bfloat16), 'group', scatter_dimension=1...]
    all_to_all x0 -> x1, starting transfers between devices: none -> 7.82 us  [shards(): lax.all_to_all(jnp.stack([w_query] * lax.axis_size('head')), 'head', 0, 0)]
  transfers between devices with their start and end apart: 4 -> 4, of which waited for: 4 -> 4; matrix products, arithmetic and copies ran while one was open for 12% -> 3% of each run, Pallas kernels for 0% -> 0%
where the time goes in v1:
time: 560 us
  waiting for transfers between devices  466 us (83%)
  starting transfers between devices  26.2 us (5%)
  matrix products  23.6 us (4%)
  local copies, waits for them, and re-layouts  19.5 us (3%)
  between operations  14.4 us (3%)
  other arithmetic  10 us (2%)
    all_gather x1, waiting for transfers between devices, shards(): whole_keyval = lax.all_gather(w_keyval, 'head', axis=0, tiled=True)  288 us
    all_to_all x1, waiting for transfers between devices, shards(): lax.all_to_all(jnp.stack([w_query] * lax.axis_size('head')), 'head', 0, 0)  107 us
    all_to_all x1, waiting for transfers between devices, shards(): lax.all_to_all(packed, 'head', split_axis=0, concat_axis=1, tiled=True)  37.6 us
    reduce_scatter x1, waiting for transfers between devices, shards(): lax.psum_scatter(total.astype(jnp.bfloat16), 'group', scatter_dimension=1...  33.2 us
    all_to_all x1, starting transfers between devices, shards(): lax.all_to_all(packed, 'head', split_axis=0, concat_axis=1, tiled=True)  18.3 us
    unnamed x22, local copies, waits for them, and re-layouts  14.1 us
  transfers between devices with their start and end apart: 4, of which 4 were waited for; matrix products, arithmetic and copies ran while one was open for 3% of the time, Pallas kernels for 0%

profile of v1, /device:TPU:8, one launch (start us, length us, event | category | flops | bytes accessed | tf_op | source)
XLA Modules:
  0.0 559.6 jit_solution(3043417986649902263)
XLA Ops:
  7.2 0.9 add_bitcast_fusion.2
  8.1 0.8 add_bitcast_fusion.1
  8.9 0.9 add_bitcast_fusion
  9.8 1.2 copy.49
  11.1 1.2 copy.51
  12.4 0.6 copy.50
  13.0 0.1 fusion.33
  13.1 0.2 fusion.18
  13.4 0.4 fusion.81
  13.7 0.2 fusion.37
  13.9 0.2 fusion.51
  14.1 0.1 fusion.32
  14.2 0.2 fusion.30
  14.5 0.3 fusion.76
  14.8 0.4 fusion.24
  15.2 0.3 convolution_convert_fusion.1
  15.5 0.3 fusion.67
  15.8 0.1 scatter-add.20
  15.9 0.1 scatter-add.25
  16.0 0.6 fusion.82
  16.6 0.5 fusion.20
  17.1 0.7 fusion.28
  17.8 0.8 fusion.25
  18.6 0.8 multiply_convert_fusion.1
  19.4 0.4 convolution_convert_fusion.2
  19.8 0.5 fusion.26
  20.4 0.8 fusion.83
  21.2 0.6 fusion.9
  21.7 0.7 fusion.8
  22.4 0.7 fusion.27
  23.1 0.7 fusion.10
  23.8 0.6 fusion.7
  24.4 0.6 convolution_convert_fusion.3
  25.0 0.7 fusion.11
  25.7 1.0 fusion.84
  26.7 0.7 fusion.3
  27.4 1.0 fusion.2
  28.5 0.9 fusion.29
  29.3 0.8 fusion.17
  30.1 0.7 multiply_convert_fusion
  30.8 0.7 convolution_convert_fusion
  31.6 0.8 fusion.16
  32.4 0.2 maximum_bitcast_fusion
  32.6 0.5 broadcast.221
  33.1 1.9 reduce.19
  35.0 1.4 reshape.251
  36.4 18.3 %all-to-all-start = ((bf16[16,2,24576]{2,1,0:T(2,128)(2,1)}), bf16[16,2,24576]{2,1,0:T(2,128)(2,1)S(1)}, u32[]{:S(2)}, u32[]{:S(2)}) async-start(bf16[16,2,24576]{2,1,0:T(2,128)(2,1)} %reshape.251), calls=%async_computation | async-start | bytes 3145728 | tf_op jit(solution)/shard_map/all_to_all | solution.py:95
  54.7 0.1 fusion.31
  54.9 37.6 %all-to-all-done = bf16[16,2,24576]{2,1,0:T(2,128)(2,1)S(1)} async-done(((bf16[16,2,24576]{2,1,0:T(2,128)(2,1)}), bf16[16,2,24576]{2,1,0:T(2,128)(2,1)S(1)}, u32[]{:S(2)}, u32[]{:S(2)}) %all-to-all-start) | async-done | bytes 1572896 | tf_op jit(solution)/shard_map/all_to_all | solution.py:95
  92.4 4.8 stack.2
  97.3 7.8 %all-to-all-start.1 = ((bf16[16,2048,128]{2,1,0:T(8,128)(2,1)}), bf16[16,2048,128]{2,1,0:T(8,128)(2,1)}, u32[]{:S(2)}, u32[]{:S(2)}) async-start(bf16[16,2048,128]{2,1,0:T(8,128)(2,1)} %stack.2), calls=%async_computation.1 | async-start | bytes 16777216 | tf_op jit(solution)/shard_map/all_to_all | solution.py:105
  105.1 0.0 all-gather.2.cloned.1.call-start
  105.2 0.6 fusion.56
  105.8 0.0 all-gather.2.cloned.1.call-update
  105.8 0.0 reduce-scatter.2.cloned.1.call-start
  105.9 8.1 %reshape.252 = bf16[2048,1,384]{2,1,0:T(2,128)(2,1)S(1)} reshape(bf16[16,2,24576]{2,1,0:T(2,128)(2,1)} %copy-done) | data formatting | bytes 3145728
  114.0 0.3 copy.71
  114.3 1.1 copy-done.1
  115.4 0.1 slice_reduce_fusion
  115.6 106.7 %all-to-all-done.1 = bf16[16,2048,128]{2,1,0:T(8,128)(2,1)} async-done(((bf16[16,2048,128]{2,1,0:T(8,128)(2,1)}), bf16[16,2048,128]{2,1,0:T(8,128)(2,1)}, u32[]{:S(2)}, u32[]{:S(2)}) %all-to-all-start.1) | async-done | bytes 8388640 | tf_op jit(solution)/shard_map/all_to_all | solution.py:105
  222.3 6.4 %fusion.12 = f32[128,2048]{1,0:T(8,128)S(1)} fusion(bf16[16,2048,128]{2,1,0:T(8,128)(2,1)} %all-to-all-done.1, bf16[128,16,384]{2,0,1:T(8,128)(2,1)} %bitcast.53), kind=kOutput, calls=%fused_computation.22 | convolution fusion | flops 1073741824 | bytes 9961472 | tf_op jit(solution)/shard_map/dot_general | solution.py:102
  228.7 288.3 %all-gather.2.cloned.1.call-done = bf16[2048,256]{1,0:T(8,128)(2,1)} async-done(((bf16[128,256]{1,0:T(8,128)(2,1)}), bf16[2048,256]{1,0:T(8,128)(2,1)}) %all-gather.2.cloned.1.call-update) | async-done | bytes 1048592 | tf_op jit(solution)/shard_map/all_gather | solution.py:111
  517.0 2.5 fusion.15
  519.5 33.2 %reduce-scatter.2.cloned.1.call-done = bf16[128,512]{1,0:T(8,128)(2,1)} async-done(((bf16[128,2048]{1,0:T(8,128)(2,1)}), bf16[128,512]{1,0:T(8,128)(2,1)}) %reduce-scatter.2.cloned.1.call-update) | async-done | bytes 131088 | tf_op jit(solution)/shard_map/reduce_scatter | solution.py:118
  (21 shorter events, 0.1 us)
Async XLA Ops:
  7.2 5.2 copy-start.2
  36.4 18.3 %copy-start.6 = (s32[64,128]{1,0:T(8,128)S(1)}, s32[64,128]{1,0:T(8,128)}, u32[]{:S(2)}) copy-start(s32[64,128]{1,0:T(8,128)} %param.37) | copy-start | bytes 98308
  36.4 18.4 %copy-start.3 = (bf16[2048,128]{1,0:T(8,128)(2,1)S(1)}, bf16[2048,128]{1,0:T(8,128)(2,1)}, u32[]{:S(2)}) copy-start(bf16[2048,128]{1,0:T(8,128)(2,1)} %param.36) | copy-start | bytes 1572868
  36.4 56.0 %all-to-all-start = ((bf16[16,2,24576]{2,1,0:T(2,128)(2,1)}), bf16[16,2,24576]{2,1,0:T(2,128)(2,1)S(1)}, u32[]{:S(2)}, u32[]{:S(2)}) async-start(bf16[16,2,24576]{2,1,0:T(2,128)(2,1)} %reshape.251), calls=%async_computation | async-start | bytes 3145728 | tf_op jit(solution)/shard_map/all_to_all | solution.py:95
  92.4 4.8 copy-start
  97.3 7.9 %copy-start.7 = (s32[4,256]{1,0:T(4,128)S(1)}, s32[4,256]{1,0:T(4,128)}, u32[]{:S(2)}) copy-start(s32[4,256]{1,0:T(4,128)} %param.39) | copy-start | bytes 12292
  97.3 7.9 %copy-start.5 = (bf16[128,256]{1,0:T(8,128)(2,1)S(1)}, bf16[128,256]{1,0:T(8,128)(2,1)}, u32[]{:S(2)}) copy-start(bf16[128,256]{1,0:T(8,128)(2,1)} %param.38) | copy-start | bytes 196612
  97.3 125.0 %all-to-all-start.1 = ((bf16[16,2048,128]{2,1,0:T(8,128)(2,1)}), bf16[16,2048,128]{2,1,0:T(8,128)(2,1)}, u32[]{:S(2)}, u32[]{:S(2)}) async-start(bf16[16,2048,128]{2,1,0:T(8,128)(2,1)} %stack.2), calls=%async_computation.1 | async-start | bytes 16777216 | tf_op jit(solution)/shard_map/all_to_all | solution.py:105
  105.1 411.9 %all-gather.2.cloned.1.call-start = ((), (), s32[]{:S(2)}) async-start(), calls=%async_computation.3 | async-start | bytes 1114112 | tf_op jit(solution)/shard_map/all_gather | solution.py:111
  105.8 446.9 %reduce-scatter.2.cloned.1.call-start = ((), (), s32[]{:S(2)}) async-start(), calls=%async_computation.4 | async-start | bytes 655360 | tf_op jit(solution)/shard_map/reduce_scatter | solution.py:118
  114.3 1.2 copy-start.1
  115.6 401.5 %copy-start.4 = (bf16[128,256]{1,0:T(8,128)(2,1)}, bf16[128,256]{1,0:T(8,128)(2,1)S(1)}, u32[]{:S(2)}) copy-start(bf16[128,256]{1,0:T(8,128)(2,1)S(1)} %slice_reduce_fusion) | copy-start | bytes 196612
Sparse Core Ops, SparseCore 0:
  109.8 407.1 all-gather.1
  520.4 32.3 reduce-scatter.1
